TPU v7x, 512 devices: a whole 4x8x8 slice. The times are simulated.
512 devices in a mesh: player: 8 (over z), feat: 64 (over y, x, core).
Axes of the slice: x: 4, y: 8, z: 8, core: 2. Of those that a mesh axis runs over, the one named last changes fastest.
Arguments:
- slab: bfloat16 [128, 524288], P(None, 'feat'), may hold values from -16 to 16
- players: bfloat16 [512, 524288], P('player', 'feat'), may hold values from -16 to 16
Outputs:
- updated: bfloat16 [512, 524288], P('player', 'feat')
All inputs are finite; a program needn't handle non-finite values.
Results may differ from a plain program's by a relative error of at most 0.0083.
Values may be sent and summed in bfloat16 or wider, within the bound.
A program may use at most 64 MiB of HBM per device.

v0:
```python
import jax
import jax.numpy as jnp
from jax import lax
from jax.sharding import Mesh
from jax.sharding import PartitionSpec as P

F = 524288
STEPS = 2
FEAT = ("feat_0", "feat_1", "feat_2")


def one_axis_at_a_time(array, axes):
    for axis in axes:
        array = lax.psum(array, axis)
    return array


def from_everyone(array, axis):
    devices = lax.axis_size(axis)
    return lax.all_to_all(
        jnp.broadcast_to(array[None], (devices, *array.shape)), axis, 0, 0, tiled=True
    )


def joined_along(tiles, dim):
    tiles = jnp.moveaxis(tiles, 0, dim)
    dims = tiles.shape
    return tiles.reshape(*dims[:dim], dims[dim] * dims[dim + 1], *dims[dim + 2 :])


def collect(array, axis, dim):
    tiles = from_everyone(array, axis)
    return joined_along(tiles, dim)


def over_copies(array, axis):
    everything = from_everyone(array, axis)
    return jnp.sum(everything, axis=0)


def on_device(slab, players):
    own_count = players.shape[0]
    k_total = own_count * lax.axis_size("player")
    first = lax.axis_index("player") * own_count
    inverse_square = 1.0 / F / F
    rows = jnp.arange(k_total, dtype=jnp.int32)[:, None]
    cols = first + jnp.arange(own_count, dtype=jnp.int32)[None, :]
    weights = players
    for step in range(STEPS):
        partial_proj = lax.dot_general(
            weights, slab, (((1,), (1,)), ((), ())), preferred_element_type=jnp.float32
        )
        proj_own = one_axis_at_a_time(partial_proj, FEAT)
        proj_all = collect(proj_own, "player", 0)
        scaled = (proj_own / F).astype(jnp.bfloat16)
        reward = jnp.dot(scaled, slab, preferred_element_type=jnp.float32)
        correlation = (
            lax.dot_general(
                proj_all, proj_own, (((1,), (1,)), ((), ())), precision=lax.Precision.HIGHEST
            )
            * inverse_square
        )
        coeff = jnp.where(rows < cols, correlation, jnp.zeros_like(correlation)).astype(
            jnp.bfloat16
        )
        penalty = lax.dot_general(
            coeff,
            lax.all_gather(weights, "player", axis=0, tiled=True),
            (((0,), (0,)), ((), ())),
            preferred_element_type=jnp.float32,
        )
        update = weights.astype(jnp.float32) + reward - penalty
        squares = jnp.sum(update * update, axis=1)
        total = over_copies(squares, FEAT)
        weights = (update * jnp.sqrt(F / (total + 1e-06))[:, None]).astype(jnp.bfloat16)
    return weights


def solution(mesh):
    split = Mesh(
        mesh.devices.reshape(mesh.shape["player"], 8, 4, 2),
        ("player", "feat_0", "feat_1", "feat_2"),
    )
    in_specs = (P(None, FEAT), P("player", FEAT))
    out_specs = P("player", FEAT)
    return jax.shard_map(
        on_device, mesh=split, in_specs=in_specs, out_specs=out_specs, check_vma=False
    )
```

profile of v0, /device:TPU:1, one launch (start us, length us, event | category | flops | bytes accessed | tf_op | source)
XLA Modules:
  0.0 279.0 jit_solution(9444974533813111568)
XLA Ops:
  6.5 0.0 copy-start
  6.5 0.7 all-gather.3.cloned.1.call-update
  7.3 0.9 copy-done
  8.1 2.2 fusion.8
  10.3 24.4 %psum.42 = f32[64,128]{1,0:T(8,128)S(1)} all-reduce(f32[64,128]{1,0:T(8,128)S(1)} %fusion.8), channel_id=1, replica_groups=mesh['player'=8,'feat_0'=8,'feat_1'=4,'feat_2'=2] {'feat_0'}, use_global_device_ids=true, to_apply=%region_0.0 | all-reduce | flops 8192 | bytes 65536 | tf_op jit(solution)/shard_map/psum | solution.py:14
  34.7 15.1 %psum.43 = f32[64,128]{1,0:T(8,128)S(1)} all-reduce(f32[64,128]{1,0:T(8,128)S(1)} %psum.42), channel_id=1, replica_groups=mesh['player'=8,'feat_0'=8,'feat_1'=4,'feat_2'=2] {'feat_1'}, use_global_device_ids=true, to_apply=%region_1.0 | all-reduce | flops 8192 | bytes 65536 | tf_op jit(solution)/shard_map/psum | solution.py:14
  49.8 12.7 %psum.44 = f32[64,128]{1,0:T(8,128)S(1)} all-reduce(f32[64,128]{1,0:T(8,128)S(1)} %psum.43), channel_id=1, replica_groups=mesh['player'=8,'feat_0'=8,'feat_1'=4,'feat_2'=2] {'feat_2'}, use_global_device_ids=true, to_apply=%region_2.0 | all-reduce | flops 8192 | bytes 65536 | tf_op jit(solution)/shard_map/psum | solution.py:14
  62.5 0.7 broadcast_in_dim.8
  63.2 10.1 %all-to-all-start = ((f32[8,64,128]{2,1,0:T(8,128)}), f32[8,64,128]{2,1,0:T(8,128)S(1)}, u32[]{:S(2)}, u32[]{:S(2)}) async-start(f32[8,64,128]{2,1,0:T(8,128)} %broadcast_in_dim.8), calls=%async_computation | async-start | bytes 524288 | tf_op jit(solution)/shard_map/all_to_all | solution.py:20
  73.3 0.0 all-gather.5.cloned.1.call-start
  73.3 1.8 convolution_add_fusion.1
  75.2 12.9 %all-to-all-done = f32[8,64,128]{2,1,0:T(8,128)S(1)} async-done(((f32[8,64,128]{2,1,0:T(8,128)}), f32[8,64,128]{2,1,0:T(8,128)S(1)}, u32[]{:S(2)}, u32[]{:S(2)}) %all-to-all-start) | async-done | bytes 262176 | tf_op jit(solution)/shard_map/all_to_all | solution.py:20
  88.1 0.4 fusion.2
  88.5 29.7 %all-gather.3.cloned.1.call-done = bf16[512,8192]{1,0:T(8,128)(2,1)} async-done(((bf16[64,8192]{1,0:T(8,128)(2,1)}), bf16[512,8192]{1,0:T(8,128)(2,1)}) %all-gather.3.cloned.1.call-update) | async-done | bytes 8388624 | tf_op jit(solution)/shard_map/all_gather | solution.py:68
  118.2 7.1 %multiply_reduce_fusion.1 = (f32[64]{0:T(128)S(1)}, f32[64,8192]{1,0:T(8,128)}) fusion(f32[64,8192]{1,0:T(8,128)} %convolution_add_fusion.1, bf16[512,64]{0,1:T(8,128)(2,1)S(1)} %fusion.2, bf16[512,8192]{1,0:T(8,128)(2,1)} %all-gather.3.cloned.1.call-done), kind=kOutput, calls=%fused_computation.7 | convolution fusion | flops 538443712 | bytes 12648704 | tf_op jit(solution)/shard_map/dot_general | solution.py:66
  125.3 19.6 %all_to_all.22 = f32[64,1,64]{2,1,0:T(1,128)S(1)} all-to-all(f32[64,1,64]{2,1,0:T(1,128)S(1)} %broadcast_in_dim.9), channel_id=1, replica_groups=mesh['player'=8,'feat_0'=8,'feat_1'=4,'feat_2'=2] {'feat_0','feat_1','fe..., dimensions={0} | all-to-all | bytes 32768 | tf_op jit(solution)/shard_map/all_to_all | solution.py:20
  144.9 2.8 multiply_convert_fusion.1
  147.7 0.0 all-gather.5.cloned.1.call-update
  147.7 0.0 copy-start.1
  147.7 2.2 fusion.9
  149.9 22.4 %psum.45 = f32[64,128]{1,0:T(8,128)S(1)} all-reduce(f32[64,128]{1,0:T(8,128)S(1)} %fusion.9), channel_id=1, replica_groups=mesh['player'=8,'feat_0'=8,'feat_1'=4,'feat_2'=2] {'feat_0'}, use_global_device_ids=true, to_apply=%region_5.6 | all-reduce | flops 8192 | bytes 65536 | tf_op jit(solution)/shard_map/psum | solution.py:14
  172.3 13.2 %psum.46 = f32[64,128]{1,0:T(8,128)S(1)} all-reduce(f32[64,128]{1,0:T(8,128)S(1)} %psum.45), channel_id=1, replica_groups=mesh['player'=8,'feat_0'=8,'feat_1'=4,'feat_2'=2] {'feat_1'}, use_global_device_ids=true, to_apply=%region_6.7 | all-reduce | flops 8192 | bytes 65536 | tf_op jit(solution)/shard_map/psum | solution.py:14
  185.5 11.4 %psum.47 = f32[64,128]{1,0:T(8,128)S(1)} all-reduce(f32[64,128]{1,0:T(8,128)S(1)} %psum.46), channel_id=1, replica_groups=mesh['player'=8,'feat_0'=8,'feat_1'=4,'feat_2'=2] {'feat_2'}, use_global_device_ids=true, to_apply=%region_7.8 | all-reduce | flops 8192 | bytes 65536 | tf_op jit(solution)/shard_map/psum | solution.py:14
  196.8 0.7 broadcast_in_dim.10
  197.6 3.9 %all-to-all-start.2 = ((f32[8,64,128]{2,1,0:T(8,128)}), f32[8,64,128]{2,1,0:T(8,128)S(1)}, u32[]{:S(2)}, u32[]{:S(2)}) async-start(f32[8,64,128]{2,1,0:T(8,128)} %broadcast_in_dim.10), calls=%async_computation.2 | async-start | bytes 524288 | tf_op jit(solution)/shard_map/all_to_all | solution.py:20
  201.4 1.8 convolution_add_fusion
  203.3 13.0 %all-to-all-done.2 = f32[8,64,128]{2,1,0:T(8,128)S(1)} async-done(((f32[8,64,128]{2,1,0:T(8,128)}), f32[8,64,128]{2,1,0:T(8,128)S(1)}, u32[]{:S(2)}, u32[]{:S(2)}) %all-to-all-start.2) | async-done | bytes 262176 | tf_op jit(solution)/shard_map/all_to_all | solution.py:20
  216.2 0.4 fusion.3
  216.7 26.0 %all-gather.5.cloned.1.call-done = bf16[512,8192]{1,0:T(8,128)(2,1)} async-done(((bf16[64,8192]{1,0:T(8,128)(2,1)}), bf16[512,8192]{1,0:T(8,128)(2,1)}) %all-gather.5.cloned.1.call-update) | async-done | bytes 8388624 | tf_op jit(solution)/shard_map/all_gather | solution.py:68
  242.7 7.1 %multiply_reduce_fusion = (f32[64]{0:T(128)S(1)}, f32[64,8192]{1,0:T(8,128)}) fusion(f32[64,8192]{1,0:T(8,128)} %convolution_add_fusion, bf16[512,64]{0,1:T(8,128)(2,1)S(1)} %fusion.3, bf16[512,8192]{1,0:T(8,128)(2,1)} %all-gather.5.cloned.1.call-done), kind=kOutput, calls=%fused_computation.5 | convolution fusion | flops 538443712 | bytes 12648704 | tf_op jit(solution)/shard_map/dot_general | solution.py:66
  249.8 19.6 %all_to_all.23 = f32[64,1,64]{2,1,0:T(1,128)S(1)} all-to-all(f32[64,1,64]{2,1,0:T(1,128)S(1)} %broadcast_in_dim.11), channel_id=1, replica_groups=mesh['player'=8,'feat_0'=8,'feat_1'=4,'feat_2'=2] {'feat_0','feat_1','fe..., dimensions={0} | all-to-all | bytes 32768 | tf_op jit(solution)/shard_map/all_to_all | solution.py:20
  269.4 2.8 multiply_convert_fusion
  (11 shorter events, 0.1 us)
Async XLA Ops:
  6.5 1.6 copy-start
  6.5 111.7 %all-gather.3.cloned.1.call-start = ((), (), s32[]{:S(2)}) async-start(), calls=%async_computation.4 | async-start | bytes 9437184 | tf_op jit(solution)/shard_map/all_gather | solution.py:68
  8.1 65.2 %copy-start.2 = (bf16[64,8192]{1,0:T(8,128)(2,1)S(1)}, bf16[64,8192]{1,0:T(8,128)(2,1)}, u32[]{:S(2)}) copy-start(bf16[64,8192]{1,0:T(8,128)(2,1)} %param.3) | copy-start | bytes 3145732
  63.2 24.9 %all-to-all-start = ((f32[8,64,128]{2,1,0:T(8,128)}), f32[8,64,128]{2,1,0:T(8,128)S(1)}, u32[]{:S(2)}, u32[]{:S(2)}) async-start(f32[8,64,128]{2,1,0:T(8,128)} %broadcast_in_dim.8), calls=%async_computation | async-start | bytes 524288 | tf_op jit(solution)/shard_map/all_to_all | solution.py:20
  73.3 169.4 %all-gather.5.cloned.1.call-start = ((), (), s32[]{:S(2)}) async-start(), calls=%async_computation.5 | async-start | bytes 9437184 | tf_op jit(solution)/shard_map/all_gather | solution.py:68
  147.7 53.7 %copy-start.1 = (bf16[64,8192]{1,0:T(8,128)(2,1)S(1)}, bf16[64,8192]{1,0:T(8,128)(2,1)}, u32[]{:S(2)}) copy-start(bf16[64,8192]{1,0:T(8,128)(2,1)} %multiply_convert_fusion.1) | copy-start | bytes 3145732
  197.6 18.7 %all-to-all-start.2 = ((f32[8,64,128]{2,1,0:T(8,128)}), f32[8,64,128]{2,1,0:T(8,128)S(1)}, u32[]{:S(2)}, u32[]{:S(2)}) async-start(f32[8,64,128]{2,1,0:T(8,128)} %broadcast_in_dim.10), calls=%async_computation.2 | async-start | bytes 524288 | tf_op jit(solution)/shard_map/all_to_all | solution.py:20
Sparse Core Ops, SparseCore 0:
  9.4 108.7 all-gather.2
  147.8 94.8 all-gather.4
where the time goes:
time: 280 us; the launch traced here: 279 us
  blocking collectives  138 us (49%)
  waiting for transfers between devices  82.4 us (29%)
  matrix products  22.9 us (8%)
  starting transfers between devices  14 us (5%)
  between operations  13.5 us (5%)
  other arithmetic  5.6 us (2%)
    psum x6, blocking collectives, one_axis_at_a_time(): array = lax.psum(array, axis)  99.1 us
    all_gather x2, waiting for transfers between devices, on_device(): lax.all_gather(weights, 'player', axis=0, tiled=True)  55.8 us
    all_to_all x2, blocking collectives, from_everyone(): lax.all_to_all(jnp.broadcast_to(array[None], (devices, *array.shape)), ax...  39.1 us
    all_to_all x2, waiting for transfers between devices, from_everyone(): lax.all_to_all(jnp.broadcast_to(array[None], (devices, *array.shape)), ax...  25.9 us
    dot_general x2, matrix products, on_device(): lax.dot_general(coeff, lax.all_gather(weights, 'player', axis=0, tiled=Tr...  14.1 us
    all_to_all x2, starting transfers between devices, from_everyone(): lax.all_to_all(jnp.broadcast_to(array[None], (devices, *array.shape)), ax...  13.9 us
  transfers between devices with their start and end apart: 4, of which 4 were waited for; matrix products, arithmetic and copies ran while one was open for 4% of the time, Pallas kernels for 0%

commit v1 on v0

v1 whole, which is shorter than its diff:
```python
import jax
import jax.numpy as jnp
from jax import lax
from jax.experimental import pallas as pl
from jax.experimental.pallas import tpu as pltpu
from jax.sharding import Mesh
from jax.sharding import PartitionSpec as P

F = 524288
EPS = 1e-06
K = 512
B = 128
OWN = 64
LOCAL = 8192
PIECE = 1024
CHUNK = 256
N = 8
AXES = ("player", "feat_0", "feat_1", "feat_2")
FEAT = AXES[1:]
MESH = pl.DeviceIdType.MESH
HIGHEST = lax.Precision.HIGHEST
F32 = jnp.float32
BF16 = jnp.bfloat16


def aligned(index, unit):
    return pl.multiple_of(index * unit, unit)


def exact_dot(a, b, dims):
    return lax.dot_general(a, b, (dims, ((), ())), precision=HIGHEST, preferred_element_type=F32)


def kernel(
    w_ref, x_ref, u_ref, scale_ref,
    wv, xv, wcat, partial, from_y, reduced, from_xc, by_z, to_y, by_y, pg, a1, m2, c2, u1, u1b, base, u2b,
    n1_a, n1_b, n1_c, n2_a, n2_b, n2_c, columns,
    load_sem, send_sem, recv_sem,
):
    z = lax.axis_index("player")
    y = lax.axis_index("feat_0")
    x = lax.axis_index("feat_1")
    c = lax.axis_index("feat_2")

    def along_z(d):
        return {"player": lax.rem(z + d, N)}

    def along_y(d):
        return {"feat_0": lax.rem(y + d, N)}

    def along_xc(d):
        return {"feat_1": lax.rem(x + d // 2, 4), "feat_2": lax.rem(c + d % 2, 2)}

    def send(src, dst, stage, device):
        pltpu.make_async_remote_copy(
            src_ref=src,
            dst_ref=dst,
            send_sem=send_sem.at[stage],
            recv_sem=recv_sem.at[stage],
            device_id=device,
            device_id_type=MESH,
        ).start()

    def wait_recv(view, stage):
        pltpu.make_async_copy(view, view, recv_sem.at[stage]).wait()

    def wait_send(view, stage):
        pltpu.make_async_copy(view, view, send_sem.at[stage]).wait()

    load_x = pltpu.make_async_copy(x_ref, xv, load_sem.at[0])
    load_w = pltpu.make_async_copy(w_ref, wv, load_sem.at[1])
    own_cols = pl.ds(aligned(z, PIECE), PIECE)
    own_rows = pl.ds(aligned(z, OWN), OWN)
    load_own = pltpu.make_async_copy(w_ref.at[:, own_cols], wcat.at[own_rows, :], load_sem.at[2])
    load_slab = pltpu.make_async_copy(x_ref.at[:, own_cols], wcat.at[pl.ds(K, B), :], load_sem.at[3])
    barrier = pltpu.get_barrier_semaphore()
    for route in (along_z, along_y, along_xc):
        for d in range(1, N):
            pl.semaphore_signal(barrier, inc=1, device_id=route(d), device_id_type=MESH)
    load_w.start()
    load_x.start()
    load_own.start()
    load_slab.start()
    pl.semaphore_wait(barrier, 3 * (N - 1))

    for d in (1, 7, 2, 6, 3, 5, 4):
        peer = lax.rem(z + d, N)
        send(w_ref.at[:, pl.ds(aligned(peer, PIECE), PIECE)], wcat.at[own_rows, :], 0, along_z(d))

    load_w.wait()
    load_x.wait()
    rows = (((1,), (1,)), ((), ()))
    own_proj = lax.dot_general(wv[...], xv[...], rows, preferred_element_type=F32)
    own_gram = lax.dot_general(xv[...], xv[...], rows, preferred_element_type=F32)
    for i in range(N):
        partial[i, 0:8] = own_proj[8 * i : 8 * i + 8]
        partial[i, 8:24] = own_gram[16 * i : 16 * i + 16]
    for d in range(1, N):
        send(partial.at[lax.rem(y + d, N)], from_y.at[d], 1, along_y(d))
    wait_recv(from_y.at[pl.ds(1, N - 1)], 1)
    total = partial[y]
    for d in range(1, N):
        total += from_y[d]
    reduced[...] = total
    for d in range(1, N):
        send(reduced, from_xc.at[d], 2, along_xc(d))
    wait_recv(from_xc.at[pl.ds(1, N - 1)], 2)
    for d in range(1, N):
        total += from_xc[d]
    by_z[z] = total[0:8]
    for d in range(1, N):
        send(by_z.at[z], by_z.at[z], 3, along_z(d))
    to_y[64:80] = total[8:24]
    wait_recv(by_z.at[pl.ds(1, N - 1)], 3)
    for i in range(N):
        to_y[8 * i : 8 * i + 8] = by_z[i]
    by_y[y] = to_y[...]
    for d in range(1, N):
        send(to_y, by_y.at[y], 4, along_y(d))
    wait_recv(by_y.at[pl.ds(1, N - 1)], 4)
    for i in range(N):
        for j in range(N):
            pg[64 * i + 8 * j : 64 * i + 8 * j + 8] = by_y[j, 8 * i : 8 * i + 8]
        pg[K + 16 * i : K + 16 * i + 16] = by_y[i, 64:80]

    earlier = lax.broadcasted_iota(jnp.int32, (K, K), 1) < lax.broadcasted_iota(jnp.int32, (K, K), 0)
    inverse_square = 1.0 / F / F
    proj = pg[0:K]
    corr = exact_dot(proj, proj, ((1,), (1,))) * inverse_square
    a1[:, 0:K] = jnp.where(earlier, -corr, 0.0).astype(BF16)
    a1[:, K : K + B] = (proj * (1.0 / F)).astype(BF16)
    proj2 = proj + exact_dot(a1[...].astype(F32), pg[...], ((1,), (0,)))
    corr2 = exact_dot(proj2, proj2, ((1,), (1,))) * inverse_square
    m2[...] = jnp.where(earlier, -corr2, 0.0)
    q2 = (proj2 * (1.0 / F)).astype(BF16)

    load_own.wait()
    load_slab.wait()
    wait_recv(wcat.at[pl.ds(0, K - OWN)], 0)

    def squares_of(value):
        wide = value * value
        return sum(wide[:, B * i : B * i + B] for i in range(CHUNK // B))

    def as_row(squares):
        return jnp.sum(jnp.transpose(squares), axis=0, keepdims=True)

    def first(i, squares):
        cols = pl.ds(aligned(i, CHUNK), CHUNK)
        value = wcat[0:K, cols].astype(F32) + jnp.dot(a1[...], wcat[:, cols], preferred_element_type=F32)
        u1[:, cols] = value
        u1b[:, cols] = value.astype(BF16)
        return squares + squares_of(value)

    squares = lax.fori_loop(0, PIECE // CHUNK, first, jnp.zeros((K, B), F32))

    def all_sum(value, bufs, stage):
        for buf, route, s in zip(bufs, (along_xc, along_y, along_z), range(stage, stage + 3)):
            buf[0] = value
            for d in range(1, N):
                send(buf.at[0], buf.at[d], s, route(d))
            if s == stage:
                yield None
            wait_recv(buf.at[pl.ds(1, N - 1)], s)
            for d in range(1, N):
                value += buf[d]
        yield value

    summing = all_sum(as_row(squares), (n1_a, n1_b, n1_c), 5)
    next(summing)

    def second_base(i, carry):
        cols = pl.ds(aligned(i, CHUNK), CHUNK)
        base[:, cols] = u1[:, cols] + jnp.dot(q2, wcat[K : K + B, cols], preferred_element_type=F32)
        return carry

    lax.fori_loop(0, PIECE // CHUNK, second_base, 0)
    n1 = next(summing)
    c2[...] = (m2[...] * (F / (n1 + EPS))).astype(BF16)

    def second(lo, hi):
        def body(i, squares):
            cols = pl.ds(aligned(i, CHUNK), CHUNK)
            value = base[lo:hi, cols] + jnp.dot(
                c2[lo:hi, 0:hi], u1b[0:hi, cols], preferred_element_type=F32
            )
            u2b[lo:hi, cols] = value.astype(BF16)
            return squares + squares_of(value)

        return lax.fori_loop(0, PIECE // CHUNK, body, jnp.zeros((hi - lo, B), F32))

    halves = [second(0, K // 2), second(K // 2, K)]
    summing = all_sum(as_row(jnp.concatenate(halves, axis=0)), (n2_a, n2_b, n2_c), 9)
    for d in (1, 7, 2, 6, 3, 5, 4):
        peer = lax.rem(z + d, N)
        send(u2b.at[pl.ds(aligned(peer, OWN), OWN), :], u_ref.at[:, own_cols], 8, along_z(d))
    keep = pltpu.make_async_copy(u2b.at[own_rows, :], u_ref.at[:, own_cols], load_sem.at[4])
    keep.start()
    next(summing)
    n2 = next(summing)
    scale = jnp.sqrt(F / (n2 + EPS * (n1 + EPS) / F))
    columns[...] = jnp.transpose(jnp.broadcast_to(scale, (B, K)))
    scale_ref[...] = columns[own_rows, :]

    wait_send(wcat.at[pl.ds(0, K - OWN)], 0)
    wait_send(from_y.at[pl.ds(1, N - 1)], 1)
    wait_send(from_xc.at[pl.ds(1, N - 1)], 2)
    wait_send(by_z.at[pl.ds(1, N - 1)], 3)
    wait_send(by_y.at[pl.ds(1, N - 1)], 4)
    for buf, stage in ((n1_a, 5), (n1_b, 6), (n1_c, 7), (n2_a, 9), (n2_b, 10), (n2_c, 11)):
        wait_send(buf.at[pl.ds(1, N - 1)], stage)
    keep.wait()
    wait_recv(u2b.at[pl.ds(0, K - OWN)], 8)
    wait_send(u2b.at[pl.ds(0, K - OWN)], 8)


def on_device(slab, players):
    def vmem(*shape, dtype=F32):
        return pltpu.VMEM(shape, dtype)

    update, scale = pl.pallas_call(
        kernel,
        out_shape=[
            jax.ShapeDtypeStruct((OWN, LOCAL), BF16),
            jax.ShapeDtypeStruct((OWN, B), F32),
        ],
        in_specs=[pl.BlockSpec(memory_space=pl.ANY)] * 2,
        out_specs=[
            pl.BlockSpec(memory_space=pl.ANY),
            pl.BlockSpec(memory_space=pltpu.VMEM),
        ],
        scratch_shapes=[
            vmem(OWN, LOCAL, dtype=BF16),
            vmem(B, LOCAL, dtype=BF16),
            vmem(K + B, PIECE, dtype=BF16),
            vmem(N, 24, B),
            vmem(N, 24, B),
            vmem(24, B),
            vmem(N, 24, B),
            vmem(N, 8, B),
            vmem(80, B),
            vmem(N, 80, B),
            vmem(K + B, B),
            vmem(K, K + B, dtype=BF16),
            vmem(K, K),
            vmem(K, K, dtype=BF16),
            vmem(K, PIECE),
            vmem(K, PIECE, dtype=BF16),
            vmem(K, PIECE),
            vmem(K, PIECE, dtype=BF16),
            *[vmem(N, 1, K) for _ in range(6)],
            vmem(K, B),
            pltpu.SemaphoreType.DMA((5,)),
            pltpu.SemaphoreType.DMA((12,)),
            pltpu.SemaphoreType.DMA((12,)),
        ],
        compiler_params=pltpu.CompilerParams(
            collective_id=0, has_side_effects=True, vmem_limit_bytes=48 * 1024 * 1024
        ),
    )(players, slab)
    return (update.astype(F32) * scale[:, 0:1]).astype(BF16)


def solution(mesh):
    split = Mesh(mesh.devices.reshape(N, 8, 4, 2), AXES)
    in_specs = (P(None, FEAT), P("player", FEAT))
    out_specs = P("player", FEAT)
    return jax.shard_map(on_device, mesh=split, in_specs=in_specs, out_specs=out_specs, check_vma=False)
```

time: 280 us -> 99.3 us (0.35)
  the two profiles are of different devices: /device:TPU:1 before, /device:TPU:2 now
where the time goes in v1:
time: 99.3 us; the launch traced here: 99.1 us
  Pallas kernels  94.9 us (96%)
  local copies, waits for them, and re-layouts  2.92 us (3%)
  other arithmetic  1.23 us (1%)
    pallas_call x1, Pallas kernels, on_device(): pl.pallas_call(kernel, out_shape=[jax.ShapeDtypeStruct((OWN, LOCAL), BF16...  94.9 us
    unnamed x4, local copies, waits for them, and re-layouts  2.81 us

profile of v1, /device:TPU:2, one launch (start us, length us, event | category | flops | bytes accessed | tf_op | source)
XLA Modules:
  0.0 99.1 jit_solution(9248790799965753667)
XLA Ops:
  0.0 0.0 copy-start
  0.0 1.6 %copy-done = bf16[128,8192]{1,0:T(8,128)(2,1)S(1)} copy-done((bf16[128,8192]{1,0:T(8,128)(2,1)S(1)}, bf16[128,8192]{1,0:T(8,128)(2,1)}, u32[]{:S(2)}) %copy-start) | copy-done | bytes 2097176
  1.6 0.0 copy-start.1
  1.6 1.2 %copy-done.1 = bf16[64,8192]{1,0:T(8,128)(2,1)S(1)} copy-done((bf16[64,8192]{1,0:T(8,128)(2,1)S(1)}, bf16[64,8192]{1,0:T(8,128)(2,1)}, u32[]{:S(2)}) %copy-start.1) | copy-done | bytes 1048600
  2.8 94.9 %shard_map.28 = (bf16[64,8192]{1,0:T(8,128)(2,1)S(1)}, f32[64,128]{1,0:T(8,128)S(1)}) custom-call(bf16[64,8192]{1,0:T(8,128)(2,1)S(1)} %copy-done.1, bf16[128,8192]{1,0:T(8,128)(2,1)S(1)} %copy-done), custom_call_target="tpu_custom_call" | custom-call | tf_op jit(solution)/shard_map/pallas_call | solution.py:221
  97.8 0.1 slice_reduce_fusion
  97.9 1.2 %multiply_convert_fusion = bf16[64,8192]{1,0:T(8,128)(2,1)} fusion(bf16[64,8192]{1,0:T(8,128)(2,1)S(1)} %get-tuple-element.7, f32[64]{0:T(128)S(1)} %slice_reduce_fusion), kind=kLoop, calls=%fused_computation | loop fusion | flops 1572864 | bytes 2097408 | tf_op jit(solution)/shard_map/convert_element_type | solution.py:261
Async XLA Ops:
  0.0 1.6 %copy-start = (bf16[128,8192]{1,0:T(8,128)(2,1)S(1)}, bf16[128,8192]{1,0:T(8,128)(2,1)}, u32[]{:S(2)}) copy-start(bf16[128,8192]{1,0:T(8,128)(2,1)} %x_ref.1) | copy-start | bytes 6291460
  1.6 1.2 %copy-start.1 = (bf16[64,8192]{1,0:T(8,128)(2,1)S(1)}, bf16[64,8192]{1,0:T(8,128)(2,1)}, u32[]{:S(2)}) copy-start(bf16[64,8192]{1,0:T(8,128)(2,1)} %w_ref.1) | copy-start | bytes 3145732

commit v2 on v1

v2 whole, which is shorter than its diff:
```python
import jax
import jax.numpy as jnp
from jax import lax
from jax.experimental import pallas as pl
from jax.experimental.pallas import tpu as pltpu
from jax.sharding import Mesh
from jax.sharding import PartitionSpec as P

F = 524288
EPS = 1e-06
K = 512
B = 128
OWN = 64
LOCAL = 8192
PIECE = 1024
CHUNK = 256
N = 8
AXES = ("player", "feat_0", "feat_1", "feat_2")
FEAT = AXES[1:]
MESH = pl.DeviceIdType.MESH
HALF = K // 2
NEAR = (1, 7, 3, 5)
FAR = (2, 6, 4)
F32 = jnp.float32
BF16 = jnp.bfloat16


def aligned(index, unit):
    return pl.multiple_of(index * unit, unit)


def halves_of(value):
    high = value.astype(BF16)
    return high, (value - high.astype(F32)).astype(BF16)


def lower_products(value, out, offset, scale, dtype):
    high, low = halves_of(value)
    left = jnp.concatenate([high, high, low], axis=1)
    right = jnp.concatenate([high, low, high], axis=1)
    for first in (0, HALF):
        size = first + HALF
        corr = lax.dot_general(
            left[first:size], right[0:size], (((1,), (1,)), ((), ())), preferred_element_type=F32
        )
        row = first + lax.broadcasted_iota(jnp.int32, corr.shape, 0)
        earlier = lax.broadcasted_iota(jnp.int32, corr.shape, 1) < row
        out[first:size, offset : offset + size] = jnp.where(earlier, corr * scale, 0.0).astype(dtype)


def kernel(
    w_ref, x_ref, u_ref, scale_ref,
    wv, xv, wcat, proj_part, proj_xc, proj_y, by_z, by_xc, gram_part, gram_xc, gram_y, gram, pg, a1, m2, c2, u1, u1b, base, u2b,
    n1_a, n1_b, n2_a, n2_b, columns,
    load_sem, send_sem, recv_sem,
):
    z = lax.axis_index("player")
    y = lax.axis_index("feat_0")
    x = lax.axis_index("feat_1")
    c = lax.axis_index("feat_2")

    def along_z(d):
        return {"player": lax.rem(z + d, N)}

    def along_y(d):
        return {"feat_0": lax.rem(y + d, N)}

    def along_xc(d):
        return {"feat_1": lax.rem(x + d // 2, 4), "feat_2": lax.rem(c + d % 2, 2)}

    def along_zc(d):
        return {"player": lax.rem(z + d // 2, N), "feat_2": lax.rem(c + d % 2, 2)}

    def along_yx(d):
        return {"feat_0": lax.rem(y + d // 4, N), "feat_1": lax.rem(x + d % 4, 4)}

    def send(src, dst, stage, device):
        pltpu.make_async_remote_copy(
            src_ref=src,
            dst_ref=dst,
            send_sem=send_sem.at[stage],
            recv_sem=recv_sem.at[stage],
            device_id=device,
            device_id_type=MESH,
        ).start()

    def wait_recv(view, stage):
        pltpu.make_async_copy(view, view, recv_sem.at[stage]).wait()

    def wait_send(view, stage):
        pltpu.make_async_copy(view, view, send_sem.at[stage]).wait()

    own_cols = pl.ds(aligned(z, PIECE), PIECE)
    own_rows = pl.ds(aligned(z, OWN), OWN)
    own_in_cat = pl.ds(aligned(z, OWN) + B, OWN)
    load_w = pltpu.make_async_copy(w_ref, wv, load_sem.at[0])
    load_x = pltpu.make_async_copy(x_ref, xv, load_sem.at[1])
    load_own = pltpu.make_async_copy(w_ref.at[:, own_cols], wcat.at[own_in_cat, :], load_sem.at[2])
    load_slab = pltpu.make_async_copy(x_ref.at[:, own_cols], wcat.at[pl.ds(0, B), :], load_sem.at[3])
    load_w.start()
    load_x.start()
    load_own.start()
    load_slab.start()
    barrier = pltpu.get_barrier_semaphore()
    for route, offsets in ((along_zc, range(1, 16)), (along_yx, range(1, 32)), (along_xc, (3, 5, 7))):
        for d in offsets:
            pl.semaphore_signal(barrier, inc=1, device_id=route(d), device_id_type=MESH)
    pl.semaphore_wait(barrier, 49)

    def send_players(offsets):
        for d in offsets:
            peer = lax.rem(z + d, N)
            send(w_ref.at[:, pl.ds(aligned(peer, PIECE), PIECE)], wcat.at[own_in_cat, :], 0, along_z(d))

    send_players(NEAR)

    own = 2 * x + c

    def piece_of(d):
        return 2 * lax.rem(x + d // 2, 4) + lax.rem(c + d % 2, 2)

    def rows_times_slab(value):
        return lax.dot_general(value, xv[...], (((1,), (1,)), ((), ())), preferred_element_type=F32)

    def added(first, buf):
        for d in range(1, N):
            first += buf[d]
        return first

    load_w.wait()
    load_x.wait()
    proj_part[...] = rows_times_slab(wv[...]).reshape(N, 8, B)
    for d in range(1, N):
        send(proj_part.at[piece_of(d)], proj_xc.at[d], 1, along_xc(d))
    gram_part[...] = rows_times_slab(xv[...]).reshape(N, 16, B)
    for d in range(1, N):
        send(gram_part.at[piece_of(d)], gram_xc.at[d], 2, along_xc(d))
    wait_recv(proj_xc.at[pl.ds(1, N - 1)], 1)
    proj_y[0] = added(proj_part[own], proj_xc)
    for d in range(1, N):
        send(proj_y.at[0], proj_y.at[d], 3, along_y(d))
    wait_recv(gram_xc.at[pl.ds(1, N - 1)], 2)
    gram_y[0] = added(gram_part[own], gram_xc)
    for d in range(1, N):
        send(gram_y.at[0], gram_y.at[d], 4, along_y(d))
    wait_recv(proj_y.at[pl.ds(1, N - 1)], 3)
    by_z[z] = added(proj_y[0], proj_y)
    for d in range(1, N):
        send(by_z.at[z], by_z.at[z], 5, along_z(d))
    send_players(FAR)
    wait_recv(gram_y.at[pl.ds(1, N - 1)], 4)
    gram[own] = added(gram_y[0], gram_y)
    for d in range(1, N):
        send(gram.at[own], gram.at[own], 6, along_xc(d))
    wait_recv(by_z.at[pl.ds(1, N - 1)], 5)
    by_xc[own] = by_z[...]
    for d in range(1, N):
        send(by_z, by_xc.at[own], 7, along_xc(d))
    wait_recv(by_xc.at[pl.ds(1, N - 1)], 7)
    for i in range(N):
        for j in range(N):
            pg[B + 64 * i + 8 * j : B + 64 * i + 8 * j + 8] = by_xc[j, i]

    inverse_square = 1.0 / F / F
    proj = pg[B : B + K]
    lower_products(proj, a1, B, -inverse_square, BF16)
    a1[:, 0:B] = (proj * (1.0 / F)).astype(BF16)

    load_own.wait()
    load_slab.wait()
    wait_recv(wcat.at[pl.ds(0, K - OWN)], 0)

    def squares_of(value):
        wide = value * value
        return sum(wide[:, B * i : B * i + B] for i in range(CHUNK // B))

    def as_row(squares):
        return jnp.sum(jnp.transpose(squares), axis=0, keepdims=True)

    squares = []
    for first in (0, HALF):
        size = first + HALF

        def body(i, total, first=first, size=size):
            cols = pl.ds(aligned(i, CHUNK), CHUNK)
            value = wcat[B + first : B + size, cols].astype(F32) + jnp.dot(
                a1[first:size, 0 : B + size], wcat[0 : B + size, cols], preferred_element_type=F32
            )
            u1[first:size, cols] = value
            u1b[first:size, cols] = value.astype(BF16)
            return total + squares_of(value)

        squares.append(lax.fori_loop(0, PIECE // CHUNK, body, jnp.zeros((HALF, B), F32), unroll=2))

    def all_sum(value, bufs, stage):
        for buf, route, s in zip(bufs, (along_zc, along_yx), (stage, stage + 1)):
            count = buf.shape[0]
            buf[0] = value
            for d in range(1, count):
                send(buf.at[0], buf.at[d], s, route(d))
            yield None
            wait_recv(buf.at[pl.ds(1, count - 1)], s)
            for d in range(1, count):
                value += buf[d]
        yield value

    summing = all_sum(as_row(jnp.concatenate(squares, axis=0)), (n1_a, n1_b), 8)
    next(summing)

    wait_recv(gram.at[pl.ds(1, N - 1)], 6)
    for i in range(N):
        pg[16 * i : 16 * i + 16] = gram[i]
    high, low = halves_of(pg[...])
    split = jnp.concatenate([high, low], axis=1)
    proj2 = []
    for first in (0, HALF):
        size = first + HALF
        terms = jnp.dot(a1[first:size, 0 : B + size], split[0 : B + size], preferred_element_type=F32)
        proj2.append(proj[first:size] + terms[:, 0:B] + terms[:, B : 2 * B])
    proj2 = jnp.concatenate(proj2, axis=0)
    lower_products(proj2, m2, 0, -inverse_square, F32)
    q2 = (proj2 * (1.0 / F)).astype(BF16)
    next(summing)

    def second_base(i, carry):
        cols = pl.ds(aligned(i, CHUNK), CHUNK)
        base[:, cols] = u1[:, cols] + jnp.dot(q2, wcat[0:B, cols], preferred_element_type=F32)
        return carry

    lax.fori_loop(0, PIECE // CHUNK, second_base, 0)
    n1 = next(summing)
    spread = F / (n1 + EPS)

    squares = []
    for first in (0, HALF):
        size = first + HALF
        c2[first:size, 0:size] = (m2[first:size, 0:size] * spread[:, 0:size]).astype(BF16)

        def body(i, total, first=first, size=size):
            cols = pl.ds(aligned(i, CHUNK), CHUNK)
            value = base[first:size, cols] + jnp.dot(
                c2[first:size, 0:size], u1b[0:size, cols], preferred_element_type=F32
            )
            u2b[first:size, cols] = value.astype(BF16)
            return total + squares_of(value)

        squares.append(lax.fori_loop(0, PIECE // CHUNK, body, jnp.zeros((HALF, B), F32), unroll=2))
    summing = all_sum(as_row(jnp.concatenate(squares, axis=0)), (n2_a, n2_b), 11)
    next(summing)
    for d in (1, 7, 2, 6, 3, 5, 4):
        peer = lax.rem(z + d, N)
        send(u2b.at[pl.ds(aligned(peer, OWN), OWN), :], u_ref.at[:, own_cols], 10, along_z(d))
    keep = pltpu.make_async_copy(u2b.at[own_rows, :], u_ref.at[:, own_cols], load_sem.at[4])
    keep.start()
    next(summing)
    n2 = next(summing)
    scale = jnp.sqrt(F / (n2 + EPS * (n1 + EPS) / F))
    columns[...] = jnp.transpose(jnp.broadcast_to(scale, (B, K)))
    scale_ref[...] = columns[own_rows, :]

    wait_send(wcat.at[pl.ds(0, K - OWN)], 0)
    for buf, stage in (
        (proj_xc, 1), (gram_xc, 2), (proj_y, 3), (gram_y, 4), (by_z, 5), (gram, 6), (by_xc, 7),
        (n1_a, 8), (n1_b, 9), (n2_a, 11), (n2_b, 12),
    ):
        wait_send(buf.at[pl.ds(1, buf.shape[0] - 1)], stage)
    keep.wait()
    wait_recv(u2b.at[pl.ds(0, K - OWN)], 10)
    wait_send(u2b.at[pl.ds(0, K - OWN)], 10)


def on_device(slab, players):
    def vmem(*shape, dtype=F32):
        return pltpu.VMEM(shape, dtype)

    update, scale = pl.pallas_call(
        kernel,
        out_shape=[
            jax.ShapeDtypeStruct((OWN, LOCAL), BF16),
            jax.ShapeDtypeStruct((OWN, B), F32),
        ],
        in_specs=[pl.BlockSpec(memory_space=pltpu.HBM)] * 2,
        out_specs=[
            pl.BlockSpec(memory_space=pl.ANY),
            pl.BlockSpec(memory_space=pltpu.VMEM),
        ],
        scratch_shapes=[
            vmem(OWN, LOCAL, dtype=BF16),
            vmem(B, LOCAL, dtype=BF16),
            vmem(B + K, PIECE, dtype=BF16),
            vmem(N, 8, B),
            vmem(N, 8, B),
            vmem(N, 8, B),
            vmem(N, 8, B),
            vmem(N, N, 8, B),
            vmem(N, 16, B),
            vmem(N, 16, B),
            vmem(N, 16, B),
            vmem(N, 16, B),
            vmem(B + K, B),
            vmem(K, B + K, dtype=BF16),
            vmem(K, K),
            vmem(K, K, dtype=BF16),
            vmem(K, PIECE),
            vmem(K, PIECE, dtype=BF16),
            vmem(K, PIECE),
            vmem(K, PIECE, dtype=BF16),
            vmem(16, 1, K),
            vmem(32, 1, K),
            vmem(16, 1, K),
            vmem(32, 1, K),
            vmem(K, B),
            pltpu.SemaphoreType.DMA((5,)),
            pltpu.SemaphoreType.DMA((13,)),
            pltpu.SemaphoreType.DMA((13,)),
        ],
        compiler_params=pltpu.CompilerParams(
            collective_id=0, has_side_effects=True, vmem_limit_bytes=48 * 1024 * 1024
        ),
    )(players, slab)
    return (update.astype(F32) * scale[:, 0:1]).astype(BF16)


def solution(mesh):
    split = Mesh(mesh.devices.reshape(N, 8, 4, 2), AXES)
    in_specs = (P(None, FEAT), P("player", FEAT))
    out_specs = P("player", FEAT)
    return jax.shard_map(on_device, mesh=split, in_specs=in_specs, out_specs=out_specs, check_vma=False)
```

time: 99.3 us -> 84.1 us (0.85)
  Pallas kernels: 94.9 us -> 79.7 us
    pallas_call x1, Pallas kernels: 94.9 us -> 79.7 us  [on_device(): pl.pallas_call(kernel, out_shape=[jax.ShapeDtypeStruct((OWN, LOCAL), BF16...]
where the time goes in v2:
time: 84.1 us; the launch traced here: 83.9 us
  Pallas kernels  79.7 us (95%)
  local copies, waits for them, and re-layouts  2.92 us (3%)
  other arithmetic  1.23 us (1%)
    pallas_call x1, Pallas kernels, on_device(): pl.pallas_call(kernel, out_shape=[jax.ShapeDtypeStruct((OWN, LOCAL), BF16...  79.7 us
    unnamed x4, local copies, waits for them, and re-layouts  2.81 us

profile of v2, /device:TPU:2, one launch (start us, length us, event | category | flops | bytes accessed | tf_op | source)
XLA Modules:
  0.0 83.9 jit_solution(5513656193501627970)
XLA Ops:
  0.0 0.0 copy-start
  0.0 1.6 %copy-done = bf16[128,8192]{1,0:T(8,128)(2,1)S(1)} copy-done((bf16[128,8192]{1,0:T(8,128)(2,1)S(1)}, bf16[128,8192]{1,0:T(8,128)(2,1)}, u32[]{:S(2)}) %copy-start) | copy-done | bytes 2097176
  1.6 0.0 copy-start.1
  1.6 1.2 %copy-done.1 = bf16[64,8192]{1,0:T(8,128)(2,1)S(1)} copy-done((bf16[64,8192]{1,0:T(8,128)(2,1)S(1)}, bf16[64,8192]{1,0:T(8,128)(2,1)}, u32[]{:S(2)}) %copy-start.1) | copy-done | bytes 1048600
  2.8 79.7 %shard_map.28 = (bf16[64,8192]{1,0:T(8,128)(2,1)S(1)}, f32[64,128]{1,0:T(8,128)S(1)}) custom-call(bf16[64,8192]{1,0:T(8,128)(2,1)S(1)} %copy-done.1, bf16[128,8192]{1,0:T(8,128)(2,1)S(1)} %copy-done), custom_call_target="tpu_custom_call" | custom-call | tf_op jit(solution)/shard_map/pallas_call | solution.py:276
  82.5 0.1 slice_reduce_fusion
  82.6 1.2 %multiply_convert_fusion = bf16[64,8192]{1,0:T(8,128)(2,1)} fusion(bf16[64,8192]{1,0:T(8,128)(2,1)S(1)} %get-tuple-element.7, f32[64]{0:T(128)S(1)} %slice_reduce_fusion), kind=kLoop, calls=%fused_computation | loop fusion | flops 1572864 | bytes 2097408 | tf_op jit(solution)/shard_map/convert_element_type | solution.py:321
Async XLA Ops:
  0.0 1.6 %copy-start = (bf16[128,8192]{1,0:T(8,128)(2,1)S(1)}, bf16[128,8192]{1,0:T(8,128)(2,1)}, u32[]{:S(2)}) copy-start(bf16[128,8192]{1,0:T(8,128)(2,1)} %x_ref.1) | copy-start | bytes 6291460
  1.6 1.2 %copy-start.1 = (bf16[64,8192]{1,0:T(8,128)(2,1)S(1)}, bf16[64,8192]{1,0:T(8,128)(2,1)}, u32[]{:S(2)}) copy-start(bf16[64,8192]{1,0:T(8,128)(2,1)} %w_ref.1) | copy-start | bytes 3145732

commit v3 on v2

--- a/solution.py
+++ b/solution.py
@@ -14,6 +14,7 @@
 LOCAL = 8192
 PIECE = 1024
 CHUNK = 256
+EARLY = 768
 N = 8
 AXES = ("player", "feat_0", "feat_1", "feat_2")
 FEAT = AXES[1:]
@@ -107,12 +108,17 @@
             pl.semaphore_signal(barrier, inc=1, device_id=route(d), device_id_type=MESH)
     pl.semaphore_wait(barrier, 49)
 
-    def send_players(offsets):
+    def send_players(offsets, begin, width, stage):
         for d in offsets:
             peer = lax.rem(z + d, N)
-            send(w_ref.at[:, pl.ds(aligned(peer, PIECE), PIECE)], wcat.at[own_in_cat, :], 0, along_z(d))
-
-    send_players(NEAR)
+            send(
+                w_ref.at[:, pl.ds(aligned(peer, PIECE) + begin, width)],
+                wcat.at[own_in_cat, pl.ds(begin, width)],
+                stage,
+                along_z(d),
+            )
+
+    send_players(NEAR, 0, PIECE, 0)
 
     own = 2 * x + c
 
@@ -147,7 +153,8 @@
     by_z[z] = added(proj_y[0], proj_y)
     for d in range(1, N):
         send(by_z.at[z], by_z.at[z], 5, along_z(d))
-    send_players(FAR)
+    send_players(FAR, 0, EARLY, 14)
+    send_players(FAR, EARLY, PIECE - EARLY, 15)
     wait_recv(gram_y.at[pl.ds(1, N - 1)], 4)
     gram[own] = added(gram_y[0], gram_y)
     for d in range(1, N):
@@ -168,7 +175,6 @@
 
     load_own.wait()
     load_slab.wait()
-    wait_recv(wcat.at[pl.ds(0, K - OWN)], 0)
 
     def squares_of(value):
         wide = value * value
@@ -177,26 +183,39 @@
     def as_row(squares):
         return jnp.sum(jnp.transpose(squares), axis=0, keepdims=True)
 
-    squares = []
-    for first in (0, HALF):
-        size = first + HALF
-
-        def body(i, total, first=first, size=size):
-            cols = pl.ds(aligned(i, CHUNK), CHUNK)
+    near = wcat.at[pl.ds(0, OWN * len(NEAR))]
+    early = wcat.at[pl.ds(0, OWN * len(FAR)), pl.ds(0, EARLY)]
+    late = wcat.at[pl.ds(0, OWN * len(FAR)), pl.ds(EARLY, PIECE - EARLY)]
+
+    def first_update(i, totals):
+        cols = pl.ds(aligned(i, CHUNK), CHUNK)
+        out = []
+        for first, total in zip((0, HALF), totals):
+            size = first + HALF
             value = wcat[B + first : B + size, cols].astype(F32) + jnp.dot(
                 a1[first:size, 0 : B + size], wcat[0 : B + size, cols], preferred_element_type=F32
             )
             u1[first:size, cols] = value
             u1b[first:size, cols] = value.astype(BF16)
-            return total + squares_of(value)
-
-        squares.append(lax.fori_loop(0, PIECE // CHUNK, body, jnp.zeros((HALF, B), F32), unroll=2))
+            out.append(total + squares_of(value))
+        return tuple(out)
+
+    wait_recv(near, 0)
+    wait_recv(early, 14)
+    squares = (jnp.zeros((HALF, B), F32),) * 2
+    squares = lax.fori_loop(0, EARLY // CHUNK, first_update, squares, unroll=True)
+    wait_recv(late, 15)
+    squares = lax.fori_loop(EARLY // CHUNK, PIECE // CHUNK, first_update, squares, unroll=True)
+
+    def hops(d, inner):
+        far, near = d // inner, d % inner
+        return min(far, N - far) + min(near, inner - near)
 
     def all_sum(value, bufs, stage):
-        for buf, route, s in zip(bufs, (along_zc, along_yx), (stage, stage + 1)):
+        for buf, route, inner, s in zip(bufs, (along_zc, along_yx), (2, 4), (stage, stage + 1)):
             count = buf.shape[0]
             buf[0] = value
-            for d in range(1, count):
+            for d in sorted(range(1, count), key=lambda d: -hops(d, inner)):
                 send(buf.at[0], buf.at[d], s, route(d))
             yield None
             wait_recv(buf.at[pl.ds(1, count - 1)], s)
@@ -231,25 +250,38 @@
     n1 = next(summing)
     spread = F / (n1 + EPS)
 
-    squares = []
     for first in (0, HALF):
         size = first + HALF
         c2[first:size, 0:size] = (m2[first:size, 0:size] * spread[:, 0:size]).astype(BF16)
 
-        def body(i, total, first=first, size=size):
-            cols = pl.ds(aligned(i, CHUNK), CHUNK)
+    def second(i, totals):
+        cols = pl.ds(aligned(i, CHUNK), CHUNK)
+        out = []
+        for first, total in zip((0, HALF), totals):
+            size = first + HALF
             value = base[first:size, cols] + jnp.dot(
                 c2[first:size, 0:size], u1b[0:size, cols], preferred_element_type=F32
             )
             u2b[first:size, cols] = value.astype(BF16)
-            return total + squares_of(value)
-
-        squares.append(lax.fori_loop(0, PIECE // CHUNK, body, jnp.zeros((HALF, B), F32), unroll=2))
+            out.append(total + squares_of(value))
+        return tuple(out)
+
+    def send_updates(begin, width, stage):
+        for d in (1, 7, 2, 6, 3, 5, 4):
+            peer = lax.rem(z + d, N)
+            send(
+                u2b.at[pl.ds(aligned(peer, OWN), OWN), pl.ds(begin, width)],
+                u_ref.at[:, pl.ds(aligned(z, PIECE) + begin, width)],
+                stage,
+                along_z(d),
+            )
+
+    squares = second(0, (jnp.zeros((HALF, B), F32),) * 2)
+    send_updates(0, CHUNK, 10)
+    squares = lax.fori_loop(1, PIECE // CHUNK, second, squares, unroll=True)
     summing = all_sum(as_row(jnp.concatenate(squares, axis=0)), (n2_a, n2_b), 11)
     next(summing)
-    for d in (1, 7, 2, 6, 3, 5, 4):
-        peer = lax.rem(z + d, N)
-        send(u2b.at[pl.ds(aligned(peer, OWN), OWN), :], u_ref.at[:, own_cols], 10, along_z(d))
+    send_updates(CHUNK, PIECE - CHUNK, 13)
     keep = pltpu.make_async_copy(u2b.at[own_rows, :], u_ref.at[:, own_cols], load_sem.at[4])
     keep.start()
     next(summing)
@@ -258,15 +290,19 @@
     columns[...] = jnp.transpose(jnp.broadcast_to(scale, (B, K)))
     scale_ref[...] = columns[own_rows, :]
 
-    wait_send(wcat.at[pl.ds(0, K - OWN)], 0)
+    wait_send(near, 0)
+    wait_send(early, 14)
+    wait_send(late, 15)
     for buf, stage in (
         (proj_xc, 1), (gram_xc, 2), (proj_y, 3), (gram_y, 4), (by_z, 5), (gram, 6), (by_xc, 7),
         (n1_a, 8), (n1_b, 9), (n2_a, 11), (n2_b, 12),
     ):
         wait_send(buf.at[pl.ds(1, buf.shape[0] - 1)], stage)
     keep.wait()
-    wait_recv(u2b.at[pl.ds(0, K - OWN)], 10)
-    wait_send(u2b.at[pl.ds(0, K - OWN)], 10)
+    for begin, width, stage in ((0, CHUNK, 10), (CHUNK, PIECE - CHUNK, 13)):
+        sent = u2b.at[pl.ds(0, K - OWN), pl.ds(begin, width)]
+        wait_recv(sent, stage)
+        wait_send(sent, stage)
 
 
 def on_device(slab, players):
@@ -311,11 +347,11 @@
             vmem(32, 1, K),
             vmem(K, B),
             pltpu.SemaphoreType.DMA((5,)),
-            pltpu.SemaphoreType.DMA((13,)),
-            pltpu.SemaphoreType.DMA((13,)),
+            pltpu.SemaphoreType.DMA((16,)),
+            pltpu.SemaphoreType.DMA((16,)),
         ],
         compiler_params=pltpu.CompilerParams(
-            collective_id=0, has_side_effects=True, vmem_limit_bytes=48 * 1024 * 1024
+            collective_id=0, has_side_effects=True, vmem_limit_bytes=60 * 1024 * 1024
         ),
     )(players, slab)
     return (update.astype(F32) * scale[:, 0:1]).astype(BF16)

time: 84.1 us -> 81.6 us (0.970)
  the two profiles are of different devices: /device:TPU:2 before, /device:TPU:64 now
where the time goes in v3:
time: 81.6 us; the launch traced here: 81.4 us
  Pallas kernels  78.1 us (96%)
  other arithmetic  2.45 us (3%)
  local copies, waits for them, and re-layouts  0.86 us (1%)
    pallas_call x1, Pallas kernels, on_device(): pl.pallas_call(kernel, out_shape=[jax.ShapeDtypeStruct((OWN, LOCAL), BF16...  78.1 us
    convert_element_type x1, other arithmetic, on_device(): return (update.astype(F32) * scale[:, 0:1]).astype(BF16)  2.45 us

profile of v3, /device:TPU:64, one launch (start us, length us, event | category | flops | bytes accessed | tf_op | source)
XLA Modules:
  0.0 81.4 jit_solution(12687135015310496386)
XLA Ops:
  0.0 78.1 %shard_map.28 = (bf16[64,8192]{1,0:T(8,128)(2,1)}, f32[64,128]{1,0:T(8,128)}) custom-call(bf16[64,8192]{1,0:T(8,128)(2,1)} %w_ref.1, bf16[128,8192]{1,0:T(8,128)(2,1)} %x_ref.1), custom_call_target="tpu_custom_call" | custom-call | tf_op jit(solution)/shard_map/pallas_call | solution.py:312
  78.1 0.9 %slice_reduce_fusion = f32[64]{0:T(128)S(1)} fusion(f32[64,128]{1,0:T(8,128)} %get-tuple-element.8), kind=kLoop, calls=%fused_computation.1 | loop fusion | bytes 512 | tf_op jit(solution)/shard_map/slice | solution.py:357
  78.9 2.4 %multiply_convert_fusion = bf16[64,8192]{1,0:T(8,128)(2,1)} fusion(bf16[64,8192]{1,0:T(8,128)(2,1)} %get-tuple-element.7, f32[64]{0:T(128)S(1)} %slice_reduce_fusion), kind=kLoop, calls=%fused_computation | loop fusion | flops 1572864 | bytes 2097408 | tf_op jit(solution)/shard_map/convert_element_type | solution.py:357

commit v4 on v3

--- a/solution.py
+++ b/solution.py
@@ -20,8 +20,8 @@
 FEAT = AXES[1:]
 MESH = pl.DeviceIdType.MESH
 HALF = K // 2
-NEAR = (1, 7, 3, 5)
-FAR = (2, 6, 4)
+NEAR = (4, 2, 6)
+FAR = (3, 5, 1, 7)
 F32 = jnp.float32
 BF16 = jnp.bfloat16
 
@@ -351,7 +351,7 @@
             pltpu.SemaphoreType.DMA((16,)),
         ],
         compiler_params=pltpu.CompilerParams(
-            collective_id=0, has_side_effects=True, vmem_limit_bytes=60 * 1024 * 1024
+            collective_id=0, has_side_effects=True, vmem_limit_bytes=52 * 1024 * 1024
         ),
     )(players, slab)
     return (update.astype(F32) * scale[:, 0:1]).astype(BF16)

time: 81.6 us -> 78.5 us (0.962)
  other arithmetic: 2.45 us -> 1.23 us
  Pallas kernels: 78.1 us -> 77 us
    convert_element_type x1, other arithmetic: 2.45 us -> 1.23 us  [on_device(): return (update.astype(F32) * scale[:, 0:1]).astype(BF16)]
    pallas_call x1, Pallas kernels: 78.1 us -> 77 us  [on_device(): pl.pallas_call(kernel, out_shape=[jax.ShapeDtypeStruct((OWN, LOCAL), BF16...]
where the time goes in v4:
time: 78.5 us; the launch traced here: 78.4 us
  Pallas kernels  77 us (98%)
  other arithmetic  1.23 us (2%)
    pallas_call x1, Pallas kernels, on_device(): pl.pallas_call(kernel, out_shape=[jax.ShapeDtypeStruct((OWN, LOCAL), BF16...  77 us

profile of v4, /device:TPU:64, one launch (start us, length us, event | category | flops | bytes accessed | tf_op | source)
XLA Modules:
  0.0 78.4 jit_solution(3451944105471111638)
XLA Ops:
  0.0 77.0 %shard_map.28 = (bf16[64,8192]{1,0:T(8,128)(2,1)S(1)}, f32[64,128]{1,0:T(8,128)S(1)}) custom-call(bf16[64,8192]{1,0:T(8,128)(2,1)} %w_ref.1, bf16[128,8192]{1,0:T(8,128)(2,1)} %x_ref.1), custom_call_target="tpu_custom_call" | custom-call | tf_op jit(solution)/shard_map/pallas_call | solution.py:312
  77.0 0.1 slice_reduce_fusion
  77.2 1.2 %multiply_convert_fusion = bf16[64,8192]{1,0:T(8,128)(2,1)} fusion(bf16[64,8192]{1,0:T(8,128)(2,1)S(1)} %get-tuple-element.7, f32[64]{0:T(128)S(1)} %slice_reduce_fusion), kind=kLoop, calls=%fused_computation | loop fusion | flops 1572864 | bytes 2097408 | tf_op jit(solution)/shard_map/convert_element_type | solution.py:357

commit v5 on v4

--- a/solution.py
+++ b/solution.py
@@ -267,7 +267,7 @@
         return tuple(out)
 
     def send_updates(begin, width, stage):
-        for d in (1, 7, 2, 6, 3, 5, 4):
+        for d in (1, 7, 4, 2, 6, 3, 5):
             peer = lax.rem(z + d, N)
             send(
                 u2b.at[pl.ds(aligned(peer, OWN), OWN), pl.ds(begin, width)],

time: 78.5 us -> 78.7 us (level)
  the two profiles are of different devices: /device:TPU:64 before, /device:TPU:1 now
where the time goes in v5:
time: 78.7 us; the launch traced here: 78.6 us
  Pallas kernels  77.2 us (98%)
  other arithmetic  1.23 us (2%)
    pallas_call x1, Pallas kernels, on_device(): pl.pallas_call(kernel, out_shape=[jax.ShapeDtypeStruct((OWN, LOCAL), BF16...  77.2 us

profile of v5, /device:TPU:1, one launch (start us, length us, event | category | flops | bytes accessed | tf_op | source)
XLA Modules:
  0.0 78.6 jit_solution(1798787363915792985)
XLA Ops:
  0.0 77.2 %shard_map.28 = (bf16[64,8192]{1,0:T(8,128)(2,1)S(1)}, f32[64,128]{1,0:T(8,128)S(1)}) custom-call(bf16[64,8192]{1,0:T(8,128)(2,1)} %w_ref.1, bf16[128,8192]{1,0:T(8,128)(2,1)} %x_ref.1), custom_call_target="tpu_custom_call" | custom-call | tf_op jit(solution)/shard_map/pallas_call | solution.py:312
  77.2 0.1 slice_reduce_fusion
  77.3 1.2 %multiply_convert_fusion = bf16[64,8192]{1,0:T(8,128)(2,1)} fusion(bf16[64,8192]{1,0:T(8,128)(2,1)S(1)} %get-tuple-element.7, f32[64]{0:T(128)S(1)} %slice_reduce_fusion), kind=kLoop, calls=%fused_computation | loop fusion | flops 1572864 | bytes 2097408 | tf_op jit(solution)/shard_map/convert_element_type | solution.py:357

commit v6 on v4

--- a/solution.py
+++ b/solution.py
@@ -14,7 +14,7 @@
 LOCAL = 8192
 PIECE = 1024
 CHUNK = 256
-EARLY = 768
+EARLY = 512
 N = 8
 AXES = ("player", "feat_0", "feat_1", "feat_2")
 FEAT = AXES[1:]

time: 78.5 us -> 78.4 us (level)
  no operation moved by 1% of the time
where the time goes in v6:
time: 78.4 us; the launch traced here: 78.3 us
  Pallas kernels  77 us (98%)
  other arithmetic  1.23 us (2%)
    pallas_call x1, Pallas kernels, on_device(): pl.pallas_call(kernel, out_shape=[jax.ShapeDtypeStruct((OWN, LOCAL), BF16...  77 us

profile of v6, /device:TPU:64, one launch (start us, length us, event | category | flops | bytes accessed | tf_op | source)
XLA Modules:
  0.0 78.3 jit_solution(12068550410978125916)
XLA Ops:
  0.0 77.0 %shard_map.28 = (bf16[64,8192]{1,0:T(8,128)(2,1)S(1)}, f32[64,128]{1,0:T(8,128)S(1)}) custom-call(bf16[64,8192]{1,0:T(8,128)(2,1)} %w_ref.1, bf16[128,8192]{1,0:T(8,128)(2,1)} %x_ref.1), custom_call_target="tpu_custom_call" | custom-call | tf_op jit(solution)/shard_map/pallas_call | solution.py:312
  77.0 0.1 slice_reduce_fusion
  77.1 1.2 %multiply_convert_fusion = bf16[64,8192]{1,0:T(8,128)(2,1)} fusion(bf16[64,8192]{1,0:T(8,128)(2,1)S(1)} %get-tuple-element.7, f32[64]{0:T(128)S(1)} %slice_reduce_fusion), kind=kLoop, calls=%fused_computation | loop fusion | flops 1572864 | bytes 2097408 | tf_op jit(solution)/shard_map/convert_element_type | solution.py:357
